TPU v7x, 32 devices: a whole 2x2x4 slice. The times are simulated.
32 devices in a mesh: seq: 8 (over z, y), head: 4 (over x, core).
Axes of the slice: x: 2, y: 2, z: 4, core: 2. Of those that a mesh axis runs over, the one named last changes fastest.
Arguments:
- layer_input: bfloat16 [4, 1024, 8192], P('head', 'seq'), may hold values from -6 to 6
- out_grad: bfloat16 [4, 1024, 8192], P('head', 'seq'), may hold values from -6 to 6
- attention_out: bfloat16 [4, 1024, 4096], P('head', 'seq'), may hold values from -6 to 6
- frozen_output_grad: bfloat16 [4, 1024, 4096], P('head', 'seq'), may hold values from -6 to 6
- query_rows: bfloat16 [4, 1024, 4096], P('head', 'seq'), may hold values from -120 to 120
- key_rows: bfloat16 [4, 1024, 512], P('head', 'seq'), may hold values from -4 to 4
- value_rows: bfloat16 [4, 1024, 512], P('head', 'seq'), may hold values from -6 to 6
- seg_lengths: int32 [4, 8], P('head'), may hold values from 1 to 256, 1024 in all within a row
- use_list: int32 [4, 8], replicated, may hold values from 0 to 31, as said below
- store_map: int32 [32], replicated, may hold values from 0 to 31, as said below
- query_down: float32 [32, 64, 8192], P('head', None, 'seq'), may hold values from -0.0625 to 0.0625
- query_up: float32 [32, 64, 4096], P('head', None, 'seq'), may hold values from -0.75 to 0.75
- output_down: float32 [32, 64, 4096], P('head', None, 'seq'), may hold values from -0.09375 to 0.09375
- output_up: float32 [32, 64, 8192], P('head', None, 'seq'), may hold values from -0.75 to 0.75
Outputs:
- grad_query_down: float32 [32, 64, 8192], P('head', None, 'seq')
- grad_query_up: float32 [32, 64, 4096], P('head', None, 'seq')
- grad_output_down: float32 [32, 64, 4096], P('head', None, 'seq')
- grad_output_up: float32 [32, 64, 8192], P('head', None, 'seq')
Inputs may be any that keep to these rules, and one draw needn't show every extreme that they name: `use_list`: each row names 8 distinct tenants. Counting a tenant's store index as store_map[tenant] // 8, a row names at most 2 tenants of one store index, and exactly 2 of some store index in every row. A permutation: tenant t's adapters are in slot store_map[t]. `seg_lengths`: each row sums to 1024.
All inputs are finite; a program needn't handle non-finite values.
Results may differ from a plain program's by a relative error of at most 0.024.
Values may be sent and summed in bfloat16 or wider, within the bound.
A program may use at most 128 MiB of HBM per device.

v0:
```python
import math
import jax
import jax.numpy as jnp
from jax import lax
from jax.sharding import PartitionSpec as P

QH = 32
KVH = 4
HD = 128
CAP = 2
adapter_scale = 2.0
big_negative = -1e30
highest = lax.Precision.HIGHEST


def contract_axes(left_side, right_side, left_dim, right_dim):
    return lax.dot_general(
        left_side,
        right_side,
        (((left_dim,), (right_dim,)), ((), ())),
        preferred_element_type=jnp.float32,
    )


def narrow(full_rows, tenant_row_mask, rank_size):
    length, used_count = tenant_row_mask.shape
    return jnp.sum(
        full_rows.reshape(length, used_count, rank_size) * tenant_row_mask[:, :, None], axis=1
    )


def widened_rows(low_rows, tenant_row_mask):
    length, used_count = tenant_row_mask.shape
    spread_rows = tenant_row_mask.astype(jnp.bfloat16)[:, :, None] * low_rows[:, None, :]
    return spread_rows.reshape(length, used_count * low_rows.shape[1])


def request_tables(use_list, store_map, slots_dev):
    tenants = store_map.shape[0]
    used_count = use_list.shape[1]
    matches = use_list[:, :, None] == jnp.arange(tenants, dtype=jnp.int32)[None, None, :]
    slot_index = jnp.sum(jnp.where(matches, store_map[None, None, :], 0), axis=2)
    owner_index = slot_index // slots_dev
    local_slot = slot_index % slots_dev
    same_owner = (owner_index[:, :, None] == owner_index[:, None, :]).astype(jnp.int32)
    indices = jnp.arange(used_count, dtype=jnp.int32)
    earlier = (indices[None, :] < indices[:, None]).astype(jnp.int32)
    rank_index = jnp.sum(same_owner * earlier[None, :, :], axis=2)
    return (owner_index, local_slot, rank_index)


def attention_grad(query_heads, key_heads, value_heads, gradient_heads, segment, key_span):
    length, head_count, head_width = query_heads.shape
    block_rows = min(512, length)
    window = block_rows + key_span
    factor = 1.0 / math.sqrt(head_width)
    padded_keys = jnp.pad(key_heads, ((key_span, 0), (0, 0), (0, 0)))
    padded_values = jnp.pad(value_heads, ((key_span, 0), (0, 0), (0, 0)))
    padded_segment = jnp.concatenate([jnp.full((key_span,), -1, jnp.int32), segment])

    def one_block(row_start):
        query_block = lax.dynamic_slice_in_dim(query_heads, row_start, block_rows, 0)
        grad_block = lax.dynamic_slice_in_dim(gradient_heads, row_start, block_rows, 0)
        key_block = lax.dynamic_slice_in_dim(padded_keys, row_start, window, 0)
        value_block = lax.dynamic_slice_in_dim(padded_values, row_start, window, 0)
        query_segment = lax.dynamic_slice_in_dim(segment, row_start, block_rows, 0)
        key_segment = lax.dynamic_slice_in_dim(padded_segment, row_start, window, 0)
        query_pos = row_start + jnp.arange(block_rows, dtype=jnp.int32)
        key_pos = row_start - key_span + jnp.arange(window, dtype=jnp.int32)
        allowed = (query_segment[:, None] == key_segment[None, :]) & (
            key_pos[None, :] <= query_pos[:, None]
        )
        scores = (
            jnp.einsum("qhd,khd->hqk", query_block, key_block, preferred_element_type=jnp.float32)
            * factor
        )
        scores = jnp.where(allowed[None, :, :], scores, big_negative)
        row_max = jnp.max(scores, axis=2, keepdims=True)
        weights = jnp.exp(scores - row_max)
        probabilities = weights / jnp.sum(weights, axis=2, keepdims=True)
        prob_grad = jnp.einsum(
            "qhd,khd->hqk", grad_block, value_block, preferred_element_type=jnp.float32
        )
        inner = jnp.sum(probabilities * prob_grad, axis=2, keepdims=True)
        score_grad = (probabilities * (prob_grad - inner)).astype(jnp.bfloat16)
        query_gradient = (
            jnp.einsum("hqk,khd->qhd", score_grad, key_block, preferred_element_type=jnp.float32)
            * factor
        )
        return query_gradient.astype(jnp.bfloat16)

    starts = jnp.arange(0, length, block_rows, dtype=jnp.int32)
    return lax.map(one_block, starts).reshape(length, head_count * head_width)


def shards(
    layer_input,
    out_grad,
    attention_out,
    frozen_output_grad,
    query_rows,
    key_rows,
    value_rows,
    seg_lengths,
    use_list,
    store_map,
    query_down,
    query_up,
    output_down,
    output_up,
):
    slots_dev = query_down.shape[0]
    rank_size = query_down.shape[1]
    group_size = QH // KVH
    input_columns, gradient_columns, head_outputs, base_heads, query_heads = (
        lax.all_to_all(layer_input[0], "seq", split_axis=1, concat_axis=0, tiled=True),
        lax.all_to_all(out_grad[0], "seq", split_axis=1, concat_axis=0, tiled=True),
        lax.all_to_all(attention_out[0], "seq", split_axis=1, concat_axis=0, tiled=True),
        lax.all_to_all(frozen_output_grad[0], "seq", split_axis=1, concat_axis=0, tiled=True),
        lax.all_to_all(query_rows[0], "seq", split_axis=1, concat_axis=0, tiled=True),
    )
    length = input_columns.shape[0]
    heads_here = query_heads.shape[1] // HD
    first_head = lax.axis_index("seq") * heads_here
    gathered_keys, gathered_values = (
        lax.all_gather(key_rows[0], "seq", axis=0, tiled=True),
        lax.all_gather(value_rows[0], "seq", axis=0, tiled=True),
    )
    kv_index = (first_head + jnp.arange(heads_here, dtype=jnp.int32)) // group_size
    key_heads = jnp.take(gathered_keys.reshape(length, KVH, HD), kv_index, axis=1)
    value_heads = jnp.take(gathered_values.reshape(length, KVH, HD), kv_index, axis=1)
    owner_index, local_slot, rank_index = request_tables(use_list, store_map, slots_dev)
    my_index = lax.axis_index("head")
    batch_count = use_list.shape[0]
    cap_ids = jnp.arange(CAP, dtype=jnp.int32)
    slot_ids = jnp.arange(slots_dev, dtype=jnp.int32)
    matched = (
        (owner_index == my_index)[:, :, None, None]
        & (rank_index[:, :, None, None] == cap_ids[None, None, :, None])
        & (local_slot[:, :, None, None] == slot_ids[None, None, None, :])
    )
    select = jnp.sum(matched.astype(jnp.float32), axis=1)

    def pack_slots(store_part):
        return jnp.einsum("mcl,lrw->mcrw", select, store_part, precision=highest).astype(
            jnp.bfloat16
        )

    fetched = (
        lax.all_to_all(pack_slots(query_down), "head", split_axis=0, concat_axis=0, tiled=True),
        lax.all_to_all(pack_slots(query_up), "head", split_axis=0, concat_axis=0, tiled=True),
        lax.all_to_all(pack_slots(output_down), "head", split_axis=0, concat_axis=0, tiled=True),
        lax.all_to_all(pack_slots(output_up), "head", split_axis=0, concat_axis=0, tiled=True),
    )
    mine_owner = lax.dynamic_index_in_dim(owner_index, my_index, 0, keepdims=False)
    mine_rank = lax.dynamic_index_in_dim(rank_index, my_index, 0, keepdims=False)
    store_ids = jnp.arange(batch_count, dtype=jnp.int32)
    picker = (
        (mine_owner[:, None, None] == store_ids[None, :, None])
        & (mine_rank[:, None, None] == cap_ids[None, None, :])
    ).astype(jnp.float32)
    picker_half = picker.astype(jnp.bfloat16)

    def unpack(received):
        chosen = jnp.einsum(
            "ijc,jcrw->irw", picker_half, received, preferred_element_type=jnp.float32
        ).astype(jnp.bfloat16)
        return chosen.reshape(chosen.shape[0] * chosen.shape[1], chosen.shape[2])

    flattened_list = [unpack(received) for received in fetched]
    lengths = seg_lengths[0]
    used_count = lengths.shape[0]
    offsets = jnp.cumsum(lengths) - lengths
    positions = jnp.arange(length, dtype=jnp.int32)
    segment = jnp.sum((positions[:, None] >= offsets[None, :]).astype(jnp.int32), axis=1) - 1
    tenant_row_mask = (segment[:, None] == jnp.arange(used_count, dtype=jnp.int32)[None, :]).astype(
        jnp.float32
    )
    partial_out = narrow(
        contract_axes(head_outputs, flattened_list[2], 1, 1), tenant_row_mask, rank_size
    )
    partial_grad = narrow(
        contract_axes(gradient_columns, flattened_list[3], 1, 1), tenant_row_mask, rank_size
    )
    partial_query = narrow(
        contract_axes(input_columns, flattened_list[0], 1, 1), tenant_row_mask, rank_size
    )
    summed_out, summed_grad, summed_query = (
        lax.psum(partial_out.astype(jnp.bfloat16), "seq").astype(jnp.float32),
        lax.psum(partial_grad.astype(jnp.bfloat16), "seq").astype(jnp.float32),
        lax.psum(partial_query.astype(jnp.bfloat16), "seq").astype(jnp.float32),
    )
    low_rank_output = summed_out.astype(jnp.bfloat16)
    low_grad = summed_grad.astype(jnp.bfloat16)
    low_rank_query = summed_query.astype(jnp.bfloat16)
    widened_gradient = widened_rows(low_grad, tenant_row_mask)
    gradient_heads = (
        base_heads.astype(jnp.float32)
        + adapter_scale
        * jnp.dot(widened_gradient, flattened_list[2], preferred_element_type=jnp.float32)
    ).astype(jnp.bfloat16)
    query_gradient = attention_grad(
        query_heads.reshape(length, heads_here, HD),
        key_heads,
        value_heads,
        gradient_heads.reshape(length, heads_here, HD),
        segment,
        length // 4,
    )
    partial_back = narrow(
        contract_axes(query_gradient, flattened_list[1], 1, 1), tenant_row_mask, rank_size
    )
    low_rank_back = lax.psum(partial_back.astype(jnp.bfloat16), "seq")
    outer_products = (
        adapter_scale
        * contract_axes(widened_rows(low_rank_back, tenant_row_mask), input_columns, 0, 0),
        adapter_scale
        * contract_axes(widened_rows(low_rank_query, tenant_row_mask), query_gradient, 0, 0),
        adapter_scale * contract_axes(widened_gradient, head_outputs, 0, 0),
        adapter_scale
        * contract_axes(widened_rows(low_rank_output, tenant_row_mask), gradient_columns, 0, 0),
    )

    def spread(gradient):
        pieces = gradient.reshape(used_count, rank_size, gradient.shape[1])
        return jnp.einsum("ijc,irw->jcrw", picker, pieces, precision=highest)

    returned = (
        lax.all_to_all(
            spread(outer_products[0]).astype(jnp.bfloat16),
            "head",
            split_axis=0,
            concat_axis=0,
            tiled=True,
        ).astype(jnp.float32),
        lax.all_to_all(
            spread(outer_products[1]).astype(jnp.bfloat16),
            "head",
            split_axis=0,
            concat_axis=0,
            tiled=True,
        ).astype(jnp.float32),
        lax.all_to_all(
            spread(outer_products[2]).astype(jnp.bfloat16),
            "head",
            split_axis=0,
            concat_axis=0,
            tiled=True,
        ).astype(jnp.float32),
        lax.all_to_all(
            spread(outer_products[3]).astype(jnp.bfloat16),
            "head",
            split_axis=0,
            concat_axis=0,
            tiled=True,
        ).astype(jnp.float32),
    )

    def settle(received):
        return jnp.einsum("mcl,mcrw->lrw", select, received, precision=highest)

    return (settle(returned[0]), settle(returned[1]), settle(returned[2]), settle(returned[3]))


def solution(mesh):
    placed = (
        P("head", "seq", None),
        P("head", "seq", None),
        P("head", "seq", None),
        P("head", "seq", None),
        P("head", "seq", None),
        P("head", "seq", None),
        P("head", "seq", None),
        P("head", None),
        P(),
        P(),
        P("head", None, "seq"),
        P("head", None, "seq"),
        P("head", None, "seq"),
        P("head", None, "seq"),
    )
    return jax.shard_map(
        shards,
        mesh=mesh,
        in_specs=placed,
        out_specs=(
            P("head", None, "seq"),
            P("head", None, "seq"),
            P("head", None, "seq"),
            P("head", None, "seq"),
        ),
        check_vma=False,
    )
```

profile of v0, /device:TPU:0, one launch (start us, length us, event | category | flops | bytes accessed | tf_op | source)
XLA Modules:
  0.0 579.0 jit_solution(9823844953946376288)
XLA Ops:
  13.1 4.2 all-to-all-start.4
  20.1 6.7 %all-to-all-done.4 = bf16[4,2,64,512]{3,1,2,0:T(2,128)(2,1)} async-done(((bf16[4,2,64,512]{3,1,2,0:T(2,128)(2,1)}), bf16[4,2,64,512]{3,1,2,0:T(2,128)(2,1)}, u32[]{:S(2)}, u32[]{:S(2)}) %all-to-all-start.4) | async-done | bytes 524320 | tf_op jit(solution)/shard_map/all_to_all | solution.py:152
  43.5 5.4 fusion.34
  50.7 7.2 %all-to-all-done.2 = bf16[4,2,64,1024]{3,1,2,0:T(2,128)(2,1)S(1)} async-done(((bf16[4,2,64,1024]{3,1,2,0:T(2,128)(2,1)}), bf16[4,2,64,1024]{3,1,2,0:T(2,128)(2,1)S(1)}, u32[]{:S(2)}, u32[]{:S(2)}) %all-to-all-start.2) | async-done | bytes 1048608 | tf_op jit(solution)/shard_map/all_to_all | solution.py:153
  63.8 13.1 %all-to-all-done.8 = bf16[4,2,64,1024]{3,1,2,0:T(2,128)(2,1)S(1)} async-done(((bf16[4,2,64,1024]{3,1,2,0:T(2,128)(2,1)}), bf16[4,2,64,1024]{3,1,2,0:T(2,128)(2,1)S(1)}, u32[]{:S(2)}, u32[]{:S(2)}) %all-to-all-start.8) | async-done | bytes 1048608 | tf_op jit(solution)/shard_map/all_to_all | solution.py:150
  77.8 6.7 %all-to-all-start.10 = ((bf16[128,8,512]{0,2,1:T(8,128)(2,1)}), bf16[128,8,512]{0,2,1:T(8,128)(2,1)S(1)}, u32[]{:S(2)}, u32[]{:S(2)}) async-start(bf16[128,8,512]{0,2,1:T(8,128)(2,1)} %bitcast.60), calls=%async_computation.10 | async-start | bytes 2097152 | tf_op jit(solution)/shard_map/all_to_all | solution.py:118
  85.8 24.3 %all-to-all-done.10 = bf16[128,8,512]{0,2,1:T(8,128)(2,1)S(1)} async-done(((bf16[128,8,512]{0,2,1:T(8,128)(2,1)}), bf16[128,8,512]{0,2,1:T(8,128)(2,1)S(1)}, u32[]{:S(2)}, u32[]{:S(2)}) %all-to-all-start.10) | async-done | bytes 1048608 | tf_op jit(solution)/shard_map/all_to_all | solution.py:118
  117.8 21.8 %all-to-all-done = bf16[128,8,512]{0,2,1:T(8,128)(2,1)S(1)} async-done(((bf16[128,8,512]{0,2,1:T(8,128)(2,1)}), bf16[128,8,512]{0,2,1:T(8,128)(2,1)S(1)}, u32[]{:S(2)}, u32[]{:S(2)}) %all-to-all-start) | async-done | bytes 1048608 | tf_op jit(solution)/shard_map/all_to_all | solution.py:120
  149.1 52.8 %all-to-all-done.3 = bf16[128,8,1024]{0,2,1:T(8,128)(2,1)S(1)} async-done(((bf16[128,8,1024]{0,2,1:T(8,128)(2,1)}), bf16[128,8,1024]{0,2,1:T(8,128)(2,1)S(1)}, u32[]{:S(2)}, u32[]{:S(2)}) %all-to-all-start.3) | async-done | bytes 2097184 | tf_op jit(solution)/shard_map/all_to_all | solution.py:117
  203.2 4.4 all-to-all-start.6
  217.7 47.6 %all-to-all-done.6 = bf16[128,8,1024]{0,2,1:T(8,128)(2,1)} async-done(((bf16[128,8,1024]{0,2,1:T(8,128)(2,1)}), bf16[128,8,1024]{0,2,1:T(8,128)(2,1)}, u32[]{:S(2)}, u32[]{:S(2)}) %all-to-all-start.6) | async-done | bytes 2097184 | tf_op jit(solution)/shard_map/all_to_all | solution.py:116
  265.3 4.5 all-to-all-start.1
  303.0 65.1 %all-reduce.7.cloned.1.call-done = bf16[1024,64]{0,1:T(8,128)(2,1)} async-done(((bf16[1024,64]{0,1:T(8,128)(2,1)}), bf16[1024,64]{0,1:T(8,128)(2,1)}) %all-reduce.7.cloned.1.call-update) | async-done | bytes 131088 | tf_op jit(solution)/shard_map/psum | solution.py:190
  371.1 50.4 %while.12 = (s32[]{:T(128)}, bf16[2,512,4,128]{3,2,1,0:T(4,128)(2,1)}, s32[2]{0:T(128)S(1)}, bf16[1280,4,128]{2,0,1:T(8,128)(2,1)S(1)}, s32[1024]{0:T(1024)S(1)}...) while((s32[]{:T(128)}, ...), condition=%wide.region_11.13_spmd, body=%wide.region_7.12_spmd.sunk | while | flops 1230110720 | bytes 50923260 | solution.py:93
  375.2 5.1 fusion.110
  382.2 7.7 %fusion.111 = (f32[4,512]{1,0:T(4,128)S(1)}, f32[4,512,768]{2,1,0:T(8,128)S(1)}) fusion(f32[4,512,768]{2,1,0:T(8,128)} %fusion.110, pred[512,768]{1,0:T(8,128)(4,1)S(1)} %compare_and_fusion.4), kind=kOutput, calls=%fused_computation.141.clone.1 | output fusion | flops 9437951 | bytes 12984320 | tf_op jit(solution)/shard_map/while/body/eval_jaxpr/sub | solution.py:79
  400.4 5.0 fusion.110
  407.3 7.7 %fusion.111 = (f32[4,512]{1,0:T(4,128)S(1)}, f32[4,512,768]{2,1,0:T(8,128)S(1)}) fusion(f32[4,512,768]{2,1,0:T(8,128)} %fusion.110, pred[512,768]{1,0:T(8,128)(4,1)S(1)} %compare_and_fusion.4), kind=kOutput, calls=%fused_computation.141.clone.1 | output fusion | flops 9437951 | bytes 12984320 | tf_op jit(solution)/shard_map/while/body/eval_jaxpr/sub | solution.py:79
  424.5 71.3 %all-reduce.9.cloned.1.call-done = (bf16[1024,64]{0,1:T(8,128)(2,1)}, bf16[1024,64]{0,1:T(8,128)(2,1)}, bf16[1024,64]{0,1:T(8,128)(2,1)}) async-done(((bf16[1024,64]{0,1:T(8,128)(2,1)}, bf16[1024,64]{0,1:T(8,128)(2,1)}, bf16[1024,64]{0,1:T(8,128)(2,1)}), (bf16[1024,64]{0,1:T(8,128)(2,1)}, bf16[1024,64]{0,1:T(8,128)(2,1)}, bf16[1024,64]{0,1:T(8,128)(2,1)})) %all-reduce.9.cloned.1.call-update) | async-done | bytes 393232 | tf_op jit(solution)/shard_map/psum | solution.py:213
  502.0 4.3 all-to-all-start.9
  510.9 4.3 all-to-all-done.9
  538.8 7.4 %all-to-all-done.12 = bf16[4,2,64,1024]{3,1,2,0:T(2,128)(2,1)S(1)} async-done(((bf16[4,2,64,1024]{3,1,2,0:T(2,128)(2,1)}), bf16[4,2,64,1024]{3,1,2,0:T(2,128)(2,1)S(1)}, u32[]{:S(2)}, u32[]{:S(2)}) %all-to-all-start.12) | async-done | bytes 1048608 | tf_op jit(solution)/shard_map/all_to_all | solution.py:250
  546.2 4.5 all-to-all-start.7
  565.2 4.3 convolution_bitcast_fusion.1
  (183 shorter events, 170.5 us)
Async XLA Ops:
  7.2 23.0 %copy-start = (f32[8,64,1024]{2,1,0:T(8,128)S(1)}, f32[8,64,1024]{2,1,0:T(8,128)}, u32[]{:S(2)}) copy-start(f32[8,64,1024]{2,1,0:T(8,128)} %param.31) | copy-start | bytes 6291460
  8.7 34.8 %copy-start.26 = (f32[4,2,8]{2,1,0:T(2,128)}, f32[4,2,8]{2,1,0:T(2,128)S(1)}, u32[]{:S(2)}) copy-start(f32[4,2,8]{2,1,0:T(2,128)S(1)} %convert_reduce_fusion.1) | copy-start | bytes 772
  13.1 13.7 %all-to-all-start.4 = ((bf16[4,2,64,512]{3,1,2,0:T(2,128)(2,1)}), bf16[4,2,64,512]{3,1,2,0:T(2,128)(2,1)}, u32[]{:S(2)}, u32[]{:S(2)}) async-start(bf16[4,2,64,512]{3,1,2,0:T(2,128)(2,1)} %copy.141), calls=%async_computation.4 | async-start | bytes 1048576 | tf_op jit(solution)/shard_map/all_to_all | solution.py:152
  26.7 12.3 %all-to-all-start.5 = ((bf16[4,2,64,512]{3,2,1,0:T(8,128)(2,1)}), bf16[4,2,64,512]{3,2,1,0:T(8,128)(2,1)S(1)}, u32[]{:S(2)}, u32[]{:S(2)}) async-start(bf16[4,2,64,512]{3,2,1,0:T(8,128)(2,1)} %copy.151), calls=%async_computation.5 | async-start | bytes 1048576 | tf_op jit(solution)/shard_map/all_to_all | solution.py:151
  39.8 18.1 %all-to-all-start.2 = ((bf16[4,2,64,1024]{3,1,2,0:T(2,128)(2,1)}), bf16[4,2,64,1024]{3,1,2,0:T(2,128)(2,1)S(1)}, u32[]{:S(2)}, u32[]{:S(2)}) async-start(bf16[4,2,64,1024]{3,1,2,0:T(2,128)(2,1)} %copy.134), calls=%async_computation.2 | async-start | bytes 2097152 | tf_op jit(solution)/shard_map/all_to_all | solution.py:153
  58.9 18.0 %all-to-all-start.8 = ((bf16[4,2,64,1024]{3,1,2,0:T(2,128)(2,1)}), bf16[4,2,64,1024]{3,1,2,0:T(2,128)(2,1)S(1)}, u32[]{:S(2)}, u32[]{:S(2)}) async-start(bf16[4,2,64,1024]{3,1,2,0:T(2,128)(2,1)} %copy.162), calls=%async_computation.8 | async-start | bytes 2097152 | tf_op jit(solution)/shard_map/all_to_all | solution.py:150
  62.5 22.1 %copy-start.11 = (bf16[1,128,4096]{2,1,0:T(8,128)(2,1)S(1)}, bf16[1,128,4096]{2,1,0:T(8,128)(2,1)}, u32[]{:S(2)}) copy-start(bf16[1,128,4096]{2,1,0:T(8,128)(2,1)} %param.22) | copy-start | bytes 3145732
  77.8 32.3 %all-to-all-start.10 = ((bf16[128,8,512]{0,2,1:T(8,128)(2,1)}), bf16[128,8,512]{0,2,1:T(8,128)(2,1)S(1)}, u32[]{:S(2)}, u32[]{:S(2)}) async-start(bf16[128,8,512]{0,2,1:T(8,128)(2,1)} %bitcast.60), calls=%async_computation.10 | async-start | bytes 2097152 | tf_op jit(solution)/shard_map/all_to_all | solution.py:118
  110.2 29.4 %all-to-all-start = ((bf16[128,8,512]{0,2,1:T(8,128)(2,1)}), bf16[128,8,512]{0,2,1:T(8,128)(2,1)S(1)}, u32[]{:S(2)}, u32[]{:S(2)}) async-start(bf16[128,8,512]{0,2,1:T(8,128)(2,1)} %bitcast.10), calls=%async_computation | async-start | bytes 2097152 | tf_op jit(solution)/shard_map/all_to_all | solution.py:120
  140.6 61.3 %all-to-all-start.3 = ((bf16[128,8,1024]{0,2,1:T(8,128)(2,1)}), bf16[128,8,1024]{0,2,1:T(8,128)(2,1)S(1)}, u32[]{:S(2)}, u32[]{:S(2)}) async-start(bf16[128,8,1024]{0,2,1:T(8,128)(2,1)} %bitcast.184), calls=%async_computation.3 | async-start | bytes 4194304 | tf_op jit(solution)/shard_map/all_to_all | solution.py:117
  144.2 131.8 %all-gather.5.cloned.1.call-start = ((), (), s32[]{:S(2)}) async-start(), calls=%async_computation.14 | async-start | bytes 1179648 | tf_op jit(solution)/shard_map/all_gather | solution.py:126
  203.2 62.1 %all-to-all-start.6 = ((bf16[128,8,1024]{0,2,1:T(8,128)(2,1)}), bf16[128,8,1024]{0,2,1:T(8,128)(2,1)}, u32[]{:S(2)}, u32[]{:S(2)}) async-start(bf16[128,8,1024]{0,2,1:T(8,128)(2,1)} %bitcast.183), calls=%async_computation.6 | async-start | bytes 4194304 | tf_op jit(solution)/shard_map/all_to_all | solution.py:116
  207.6 70.1 %all-gather.7.cloned.1.call-start = ((), (), s32[]{:S(2)}) async-start(), calls=%async_computation.15 | async-start | bytes 1179648 | tf_op jit(solution)/shard_map/all_gather | solution.py:127
  215.5 54.8 %copy-start.14 = (bf16[4,2,64,1024]{3,1,2,0:T(2,128)(2,1)S(1)}, bf16[4,2,64,1024]{3,1,2,0:T(2,128)(2,1)}, u32[]{:S(2)}) copy-start(bf16[4,2,64,1024]{3,1,2,0:T(2,128)(2,1)} %copy-done.13) | copy-start | bytes 3145732
  265.3 37.7 %all-to-all-start.1 = ((bf16[128,8,512]{0,2,1:T(8,128)(2,1)}), bf16[128,8,512]{0,2,1:T(8,128)(2,1)}, u32[]{:S(2)}, u32[]{:S(2)}) async-start(bf16[128,8,512]{0,2,1:T(8,128)(2,1)} %bitcast.12), calls=%async_computation.1 | async-start | bytes 2097152 | tf_op jit(solution)/shard_map/all_to_all | solution.py:119
  269.9 98.3 %all-reduce.7.cloned.1.call-start = ((), (), s32[]{:S(2)}) async-start(), calls=%async_computation.13 | async-start | bytes 262144 | tf_op jit(solution)/shard_map/psum | solution.py:190
  297.9 197.9 %all-reduce.9.cloned.1.call-start = ((), (), s32[]{:S(2)}) async-start(), calls=%async_computation.16 | async-start | bytes 786432 | tf_op jit(solution)/shard_map/psum | solution.py:213
  300.9 67.2 %copy-start.22 = (bf16[8,64,512]{2,0,1:T(8,128)(2,1)S(1)}, bf16[8,64,512]{2,0,1:T(8,128)(2,1)}, u32[]{:S(2)}) copy-start(bf16[8,64,512]{2,0,1:T(8,128)(2,1)} %copy-done.21) | copy-start | bytes 1572868
  423.0 72.8 %copy-start.23 = (bf16[1024,64]{0,1:T(8,128)(2,1)S(1)}, bf16[1024,64]{0,1:T(8,128)(2,1)}, u32[]{:S(2)}) copy-start(bf16[1024,64]{0,1:T(8,128)(2,1)} %all-reduce.7.cloned.1.call-done) | copy-start | bytes 393220
  502.0 13.2 %all-to-all-start.9 = ((bf16[4,2,64,512]{3,1,2,0:T(2,128)(2,1)}), bf16[4,2,64,512]{3,1,2,0:T(2,128)(2,1)}, u32[]{:S(2)}, u32[]{:S(2)}) async-start(bf16[4,2,64,512]{3,1,2,0:T(2,128)(2,1)} %copy.166), calls=%async_computation.9 | async-start | bytes 1048576 | tf_op jit(solution)/shard_map/all_to_all | solution.py:236
  515.2 13.0 %all-to-all-start.11 = ((bf16[4,2,64,512]{3,1,2,0:T(2,128)(2,1)}), bf16[4,2,64,512]{3,1,2,0:T(2,128)(2,1)}, u32[]{:S(2)}, u32[]{:S(2)}) async-start(bf16[4,2,64,512]{3,1,2,0:T(2,128)(2,1)} %copy.172), calls=%async_computation.11 | async-start | bytes 1048576 | tf_op jit(solution)/shard_map/all_to_all | solution.py:243
  528.3 18.0 %all-to-all-start.12 = ((bf16[4,2,64,1024]{3,1,2,0:T(2,128)(2,1)}), bf16[4,2,64,1024]{3,1,2,0:T(2,128)(2,1)S(1)}, u32[]{:S(2)}, u32[]{:S(2)}) async-start(bf16[4,2,64,1024]{3,1,2,0:T(2,128)(2,1)} %copy.177), calls=%async_computation.12 | async-start | bytes 2097152 | tf_op jit(solution)/shard_map/all_to_all | solution.py:250
  537.1 13.7 %copy-start.27 = (f32[4,2,8]{2,1,0:T(2,128)S(1)}, f32[4,2,8]{2,1,0:T(2,128)}, u32[]{:S(2)}) copy-start(f32[4,2,8]{2,1,0:T(2,128)} %copy-done.26) | copy-start | bytes 772
  546.2 19.0 %all-to-all-start.7 = ((bf16[4,2,64,1024]{3,1,2,0:T(2,128)(2,1)}), bf16[4,2,64,1024]{3,1,2,0:T(2,128)(2,1)}, u32[]{:S(2)}, u32[]{:S(2)}) async-start(bf16[4,2,64,1024]{3,1,2,0:T(2,128)(2,1)} %copy.157), calls=%async_computation.7 | async-start | bytes 2097152 | tf_op jit(solution)/shard_map/all_to_all | solution.py:229
  (23 other events, 106.6 us)
Sparse Core Ops, SparseCore 0:
  147.1 61.6 all-gather.4
  210.9 61.0 all-gather.6
  298.0 70.0 all-reduce.6
  424.6 71.1 all-reduce.8
where the time goes:
time: 588 us; the launch traced here: 579 us
  waiting for transfers between devices  329 us (56%)
  matrix products  79.1 us (13%)
  local copies, waits for them, and re-layouts  67.7 us (12%)
  starting transfers between devices  54.7 us (9%)
  other arithmetic  25.2 us (4%)
  between operations  14.8 us (3%)
  loops' own time  8.21 us (1%)
    psum x1, waiting for transfers between devices, shards(): low_rank_back = lax.psum(partial_back.astype(jnp.bfloat16), 'seq')  71.3 us
    psum x1, waiting for transfers between devices, shards(): lax.psum(partial_grad.astype(jnp.bfloat16), 'seq').astype(jnp.float32)  65.1 us
    all_to_all x1, waiting for transfers between devices, shards(): lax.all_to_all(out_grad[0], 'seq', split_axis=1, concat_axis=0, tiled=True)  52.8 us
    all_to_all x1, waiting for transfers between devices, shards(): lax.all_to_all(layer_input[0], 'seq', split_axis=1, concat_axis=0, tiled=...  47.6 us
    unnamed x71, local copies, waits for them, and re-layouts  28.1 us
    all_to_all x1, waiting for transfers between devices, shards(): lax.all_to_all(attention_out[0], 'seq', split_axis=1, concat_axis=0, tile...  24.3 us
    all_to_all x1, waiting for transfers between devices, shards(): lax.all_to_all(query_rows[0], 'seq', split_axis=1, concat_axis=0, tiled=T...  21.8 us
    sub x2, other arithmetic, one_block(): weights = jnp.exp(scores - row_max)  15.4 us
  transfers between devices with their start and end apart: 17, of which 14 were waited for; matrix products, arithmetic and copies ran while one was open for 17% of the time, Pallas kernels for 0%

commit v1 on v0

--- a/solution.py
+++ b/solution.py
@@ -11,6 +11,26 @@
 adapter_scale = 2.0
 big_negative = -1e30
 highest = lax.Precision.HIGHEST
+
+
+def update_the_shifts_all(m):
+    vec_out, newest = (lax.psum(1, "head"), lax.axis_index("head"))
+    v1 = list(m.shape)
+    z2 = m.shape[0] // vec_out
+    v1[0] = z2
+    spare = v1[0]
+    v1[0] = spare * vec_out
+    part_now = jnp.zeros(v1, m.dtype)
+    for rr in range(vec_out):
+        state_next = lax.dynamic_slice_in_dim(m, (newest ^ rr) * z2, z2, axis=0)
+        if rr:
+            state_next = lax.ppermute(
+                state_next, "head", list(map(lambda q: (q, q ^ rr), range(vec_out)))
+            )
+        part_now = lax.dynamic_update_slice_in_dim(
+            part_now, state_next, (newest ^ rr) * spare, axis=0
+        )
+    return part_now
 
 
 def contract_axes(left_side, right_side, left_dim, right_dim):
@@ -147,7 +167,7 @@
         )
 
     fetched = (
-        lax.all_to_all(pack_slots(query_down), "head", split_axis=0, concat_axis=0, tiled=True),
+        update_the_shifts_all(pack_slots(query_down)),
         lax.all_to_all(pack_slots(query_up), "head", split_axis=0, concat_axis=0, tiled=True),
         lax.all_to_all(pack_slots(output_down), "head", split_axis=0, concat_axis=0, tiled=True),
         lax.all_to_all(pack_slots(output_up), "head", split_axis=0, concat_axis=0, tiled=True),

time: 588 us -> 576 us (0.980)
  waiting for transfers between devices: 329 us -> 301 us
  local copies, waits for them, and re-layouts: 67.7 us -> 86.9 us
    all_to_all x1, waiting for transfers between devices: 52.8 us -> 6.77 us  [shards(): lax.all_to_all(out_grad[0], 'seq', split_axis=1, concat_axis=0, tiled=True)]
    dynamic_update_slice x0 -> x4, local copies, waits for them, and re-layouts: none -> 13.5 us  [update_the_shifts_all(): lax.dynamic_update_slice_in_dim(part_now, state_next, (newest ^ rr) * spa...]
    all_to_all x1 -> x0, waiting for transfers between devices: 13.1 us -> none  [shards(): lax.all_to_all(pack_slots(query_down), 'head', split_axis=0, concat_axis=...]
    all_gather x1, waiting for transfers between devices: 0.02 us -> 9.87 us  [shards(): lax.all_gather(value_rows[0], 'seq', axis=0, tiled=True)]
    ppermute x0 -> x3, waiting for transfers between devices: none -> 6.48 us  [update_the_shifts_all(): lax.ppermute(state_next, 'head', list(map(lambda q: (q, q ^ rr), range(ve...]
    all_to_all x1, waiting for transfers between devices: 7.22 us -> 13.1 us  [shards(): lax.all_to_all(pack_slots(output_up), 'head', split_axis=0, concat_axis=0...]
    unnamed x71 -> x63, local copies, waits for them, and re-layouts: 28.1 us -> 26.4 us
  transfers between devices with their start and end apart: 17 -> 19, of which waited for: 14 -> 16; matrix products, arithmetic and copies ran while one was open for 17% -> 21% of each run, Pallas kernels for 0% -> 0%
where the time goes in v1:
time: 576 us; the launch traced here: 566 us
  waiting for transfers between devices  301 us (52%)
  local copies, waits for them, and re-layouts  86.9 us (15%)
  matrix products  77.7 us (13%)
  starting transfers between devices  52.4 us (9%)
  other arithmetic  25.1 us (4%)
  between operations  14.9 us (3%)
  loops' own time  7.6 us (1%)
    psum x1, waiting for transfers between devices, shards(): low_rank_back = lax.psum(partial_back.astype(jnp.bfloat16), 'seq')  71.3 us
    psum x1, waiting for transfers between devices, shards(): lax.psum(partial_grad.astype(jnp.bfloat16), 'seq').astype(jnp.float32)  68.7 us
    all_to_all x1, waiting for transfers between devices, shards(): lax.all_to_all(layer_input[0], 'seq', split_axis=1, concat_axis=0, tiled=...  52.8 us
    unnamed x63, local copies, waits for them, and re-layouts  26.4 us
    all_to_all x1, waiting for transfers between devices, shards(): lax.all_to_all(attention_out[0], 'seq', split_axis=1, concat_axis=0, tile...  24.3 us
    all_to_all x1, waiting for transfers between devices, shards(): lax.all_to_all(query_rows[0], 'seq', split_axis=1, concat_axis=0, tiled=T...  21.8 us
    sub x2, other arithmetic, one_block(): weights = jnp.exp(scores - row_max)  15.4 us
    dot_general x8, matrix products, contract_axes(): lax.dot_general(left_side, right_side, (((left_dim,), (right_dim,)), ((),...  14.5 us
  transfers between devices with their start and end apart: 19, of which 16 were waited for; matrix products, arithmetic and copies ran while one was open for 21% of the time, Pallas kernels for 0%

profile of v1, /device:TPU:0, one launch (start us, length us, event | category | flops | bytes accessed | tf_op | source)
XLA Modules:
  0.0 565.7 jit_solution(8817174560100492129)
XLA Ops:
  20.0 6.7 %all-to-all-done.4 = bf16[4,2,64,512]{3,1,2,0:T(2,128)(2,1)} async-done(((bf16[4,2,64,512]{3,1,2,0:T(2,128)(2,1)}), bf16[4,2,64,512]{3,1,2,0:T(2,128)(2,1)}, u32[]{:S(2)}, u32[]{:S(2)}) %all-to-all-start.4) | async-done | bytes 524320 | tf_op jit(solution)/shard_map/all_to_all | solution.py:172
  44.7 13.1 %all-to-all-done.2 = bf16[4,2,64,1024]{3,1,2,0:T(2,128)(2,1)S(1)} async-done(((bf16[4,2,64,1024]{3,1,2,0:T(2,128)(2,1)}), bf16[4,2,64,1024]{3,1,2,0:T(2,128)(2,1)S(1)}, u32[]{:S(2)}, u32[]{:S(2)}) %all-to-all-start.2) | async-done | bytes 1048608 | tf_op jit(solution)/shard_map/all_to_all | solution.py:173
  58.7 6.7 %all-to-all-start.9 = ((bf16[128,8,512]{0,2,1:T(8,128)(2,1)}), bf16[128,8,512]{0,2,1:T(8,128)(2,1)S(1)}, u32[]{:S(2)}, u32[]{:S(2)}) async-start(bf16[128,8,512]{0,2,1:T(8,128)(2,1)} %bitcast.60), calls=%async_computation.9 | async-start | bytes 2097152 | tf_op jit(solution)/shard_map/all_to_all | solution.py:138
  66.7 24.3 %all-to-all-done.9 = bf16[128,8,512]{0,2,1:T(8,128)(2,1)S(1)} async-done(((bf16[128,8,512]{0,2,1:T(8,128)(2,1)}), bf16[128,8,512]{0,2,1:T(8,128)(2,1)S(1)}, u32[]{:S(2)}, u32[]{:S(2)}) %all-to-all-start.9) | async-done | bytes 1048608 | tf_op jit(solution)/shard_map/all_to_all | solution.py:138
  98.7 21.8 %all-to-all-done = bf16[128,8,512]{0,2,1:T(8,128)(2,1)S(1)} async-done(((bf16[128,8,512]{0,2,1:T(8,128)(2,1)}), bf16[128,8,512]{0,2,1:T(8,128)(2,1)S(1)}, u32[]{:S(2)}, u32[]{:S(2)}) %all-to-all-start) | async-done | bytes 1048608 | tf_op jit(solution)/shard_map/all_to_all | solution.py:140
  130.0 52.8 %all-to-all-done.6 = bf16[128,8,1024]{0,2,1:T(8,128)(2,1)S(1)} async-done(((bf16[128,8,1024]{0,2,1:T(8,128)(2,1)}), bf16[128,8,1024]{0,2,1:T(8,128)(2,1)S(1)}, u32[]{:S(2)}, u32[]{:S(2)}) %all-to-all-start.6) | async-done | bytes 2097184 | tf_op jit(solution)/shard_map/all_to_all | solution.py:136
  184.1 4.6 all-to-all-start.3
  188.8 5.4 fusion.35
  217.4 5.5 collective-permute-done.2
  234.4 6.8 %all-to-all-done.3 = bf16[128,8,1024]{0,2,1:T(8,128)(2,1)} async-done(((bf16[128,8,1024]{0,2,1:T(8,128)(2,1)}), bf16[128,8,1024]{0,2,1:T(8,128)(2,1)}, u32[]{:S(2)}, u32[]{:S(2)}) %all-to-all-start.3) | async-done | bytes 2097184 | tf_op jit(solution)/shard_map/all_to_all | solution.py:137
  241.2 4.3 all-to-all-start.1
  251.7 9.9 %all-gather.7.cloned.1.call-done = bf16[1,1024,512]{1,2,0:T(8,128)(2,1)} async-done(((bf16[1,128,512]{1,2,0:T(8,128)(2,1)}), bf16[1,1024,512]{1,2,0:T(8,128)(2,1)}) %all-gather.7.cloned.1.call-update) | async-done | bytes 1048592 | tf_op jit(solution)/shard_map/all_gather | solution.py:147
  286.9 68.7 %all-reduce.7.cloned.1.call-done = bf16[1024,64]{0,1:T(8,128)(2,1)} async-done(((bf16[1024,64]{0,1:T(8,128)(2,1)}), bf16[1024,64]{0,1:T(8,128)(2,1)}) %all-reduce.7.cloned.1.call-update) | async-done | bytes 131088 | tf_op jit(solution)/shard_map/psum | solution.py:210
  358.6 49.6 %while.12 = (s32[]{:T(128)}, bf16[2,512,4,128]{3,2,1,0:T(4,128)(2,1)}, s32[2]{0:T(128)S(1)}, bf16[1280,4,128]{2,0,1:T(8,128)(2,1)S(1)}, s32[1024]{0:T(1024)S(1)}...) while((s32[]{:T(128)}, ...), condition=%wide.region_11.13_spmd, body=%wide.region_7.12_spmd.sunk | while | flops 1230110720 | bytes 50923260 | solution.py:113
  362.3 5.1 fusion.112
  369.2 7.7 %fusion.113 = (f32[4,512]{1,0:T(4,128)S(1)}, f32[4,512,768]{2,1,0:T(8,128)S(1)}) fusion(f32[4,512,768]{2,1,0:T(8,128)} %fusion.112, pred[512,768]{1,0:T(8,128)(4,1)S(1)} %compare_and_fusion.4), kind=kOutput, calls=%fused_computation.146.clone.1 | output fusion | flops 9437951 | bytes 12984320 | tf_op jit(solution)/shard_map/while/body/eval_jaxpr/sub | solution.py:99
  387.1 5.1 fusion.112
  394.0 7.7 %fusion.113 = (f32[4,512]{1,0:T(4,128)S(1)}, f32[4,512,768]{2,1,0:T(8,128)S(1)}) fusion(f32[4,512,768]{2,1,0:T(8,128)} %fusion.112, pred[512,768]{1,0:T(8,128)(4,1)S(1)} %compare_and_fusion.4), kind=kOutput, calls=%fused_computation.146.clone.1 | output fusion | flops 9437951 | bytes 12984320 | tf_op jit(solution)/shard_map/while/body/eval_jaxpr/sub | solution.py:99
  411.2 71.3 %all-reduce.9.cloned.1.call-done = (bf16[1024,64]{0,1:T(8,128)(2,1)}, bf16[1024,64]{0,1:T(8,128)(2,1)}, bf16[1024,64]{0,1:T(8,128)(2,1)}) async-done(((bf16[1024,64]{0,1:T(8,128)(2,1)}, bf16[1024,64]{0,1:T(8,128)(2,1)}, bf16[1024,64]{0,1:T(8,128)(2,1)}), (bf16[1024,64]{0,1:T(8,128)(2,1)}, bf16[1024,64]{0,1:T(8,128)(2,1)}, bf16[1024,64]{0,1:T(8,128)(2,1)})) %all-reduce.9.cloned.1.call-update) | async-done | bytes 393232 | tf_op jit(solution)/shard_map/psum | solution.py:233
  488.6 4.4 all-to-all-start.8
  497.6 4.3 all-to-all-done.8
  525.5 7.4 %all-to-all-done.11 = bf16[4,2,64,1024]{3,1,2,0:T(2,128)(2,1)S(1)} async-done(((bf16[4,2,64,1024]{3,1,2,0:T(2,128)(2,1)}), bf16[4,2,64,1024]{3,1,2,0:T(2,128)(2,1)S(1)}, u32[]{:S(2)}, u32[]{:S(2)}) %all-to-all-start.11) | async-done | bytes 1048608 | tf_op jit(solution)/shard_map/all_to_all | solution.py:270
  532.9 4.5 all-to-all-start.7
  551.9 4.3 convolution_bitcast_fusion.1
  (188 shorter events, 191.1 us)
Async XLA Ops:
  7.2 23.0 %copy-start = (f32[8,64,1024]{2,1,0:T(8,128)S(1)}, f32[8,64,1024]{2,1,0:T(8,128)}, u32[]{:S(2)}) copy-start(f32[8,64,1024]{2,1,0:T(8,128)} %param.31) | copy-start | bytes 6291460
  13.0 13.7 %all-to-all-start.4 = ((bf16[4,2,64,512]{3,1,2,0:T(2,128)(2,1)}), bf16[4,2,64,512]{3,1,2,0:T(2,128)(2,1)}, u32[]{:S(2)}, u32[]{:S(2)}) async-start(bf16[4,2,64,512]{3,1,2,0:T(2,128)(2,1)} %copy.157), calls=%async_computation.4 | async-start | bytes 1048576 | tf_op jit(solution)/shard_map/all_to_all | solution.py:172
  26.7 12.3 %all-to-all-start.5 = ((bf16[4,2,64,512]{3,2,1,0:T(8,128)(2,1)}), bf16[4,2,64,512]{3,2,1,0:T(8,128)(2,1)S(1)}, u32[]{:S(2)}, u32[]{:S(2)}) async-start(bf16[4,2,64,512]{3,2,1,0:T(8,128)(2,1)} %copy.167), calls=%async_computation.5 | async-start | bytes 1048576 | tf_op jit(solution)/shard_map/all_to_all | solution.py:171
  39.8 18.0 %all-to-all-start.2 = ((bf16[4,2,64,1024]{3,1,2,0:T(2,128)(2,1)}), bf16[4,2,64,1024]{3,1,2,0:T(2,128)(2,1)S(1)}, u32[]{:S(2)}, u32[]{:S(2)}) async-start(bf16[4,2,64,1024]{3,1,2,0:T(2,128)(2,1)} %copy.150), calls=%async_computation.2 | async-start | bytes 2097152 | tf_op jit(solution)/shard_map/all_to_all | solution.py:173
  43.3 22.1 %copy-start.11 = (bf16[1,128,4096]{2,1,0:T(8,128)(2,1)S(1)}, bf16[1,128,4096]{2,1,0:T(8,128)(2,1)}, u32[]{:S(2)}) copy-start(bf16[1,128,4096]{2,1,0:T(8,128)(2,1)} %param.22) | copy-start | bytes 3145732
  58.7 32.3 %all-to-all-start.9 = ((bf16[128,8,512]{0,2,1:T(8,128)(2,1)}), bf16[128,8,512]{0,2,1:T(8,128)(2,1)S(1)}, u32[]{:S(2)}, u32[]{:S(2)}) async-start(bf16[128,8,512]{0,2,1:T(8,128)(2,1)} %bitcast.60), calls=%async_computation.9 | async-start | bytes 2097152 | tf_op jit(solution)/shard_map/all_to_all | solution.py:138
  91.1 29.4 %all-to-all-start = ((bf16[128,8,512]{0,2,1:T(8,128)(2,1)}), bf16[128,8,512]{0,2,1:T(8,128)(2,1)S(1)}, u32[]{:S(2)}, u32[]{:S(2)}) async-start(bf16[128,8,512]{0,2,1:T(8,128)(2,1)} %bitcast.10), calls=%async_computation | async-start | bytes 2097152 | tf_op jit(solution)/shard_map/all_to_all | solution.py:140
  121.5 61.3 %all-to-all-start.6 = ((bf16[128,8,1024]{0,2,1:T(8,128)(2,1)}), bf16[128,8,1024]{0,2,1:T(8,128)(2,1)S(1)}, u32[]{:S(2)}, u32[]{:S(2)}) async-start(bf16[128,8,1024]{0,2,1:T(8,128)(2,1)} %bitcast.187), calls=%async_computation.6 | async-start | bytes 4194304 | tf_op jit(solution)/shard_map/all_to_all | solution.py:136
  125.1 125.0 %all-gather.5.cloned.1.call-start = ((), (), s32[]{:S(2)}) async-start(), calls=%async_computation.13 | async-start | bytes 1179648 | tf_op jit(solution)/shard_map/all_gather | solution.py:146
  184.1 57.0 %all-to-all-start.3 = ((bf16[128,8,1024]{0,2,1:T(8,128)(2,1)}), bf16[128,8,1024]{0,2,1:T(8,128)(2,1)}, u32[]{:S(2)}, u32[]{:S(2)}) async-start(bf16[128,8,1024]{0,2,1:T(8,128)(2,1)} %bitcast.186), calls=%async_computation.3 | async-start | bytes 4194304 | tf_op jit(solution)/shard_map/all_to_all | solution.py:137
  188.7 72.9 %all-gather.7.cloned.1.call-start = ((), (), s32[]{:S(2)}) async-start(), calls=%async_computation.14 | async-start | bytes 1179648 | tf_op jit(solution)/shard_map/all_gather | solution.py:147
  197.4 9.1 %collective-permute-start = (bf16[1,2,64,1024]{3,0,2,1:T(2,128)(2,1)}, bf16[1,2,64,1024]{3,0,2,1:T(2,128)(2,1)}, u32[]{:S(2)}, u32[]{:S(2)}) collective-permute-start(bf16[1,2,64,1024]{3,0,2,1:T(2,128)(2,1)} %get-tuple-element.216), channel_id=1, source_target_pairs={{0,1},{1,0},{2,3},{3,2},{4,5},{5,4},{6,7},{7,6},{8,9},{9,8},{10,11... | collective-permute-start | bytes 786440 | tf_op jit(solution)/shard_map/ppermute | solution.py:27
  197.4 15.0 %collective-permute-start.1 = (bf16[1,2,64,1024]{3,0,2,1:T(2,128)(2,1)}, bf16[1,2,64,1024]{3,0,2,1:T(2,128)(2,1)}, u32[]{:S(2)}, u32[]{:S(2)}) collective-permute-start(bf16[1,2,64,1024]{3,0,2,1:T(2,128)(2,1)} %get-tuple-element.215), channel_id=1, source_target_pairs={{0,2},{1,3},{2,0},{3,1},{4,6},{5,7},{6,4},{7,5},{8,10},{9,11},{10,... | collective-permute-start | bytes 786440 | tf_op jit(solution)/shard_map/ppermute | solution.py:27
  198.7 24.1 %collective-permute-start.2 = (bf16[1,2,64,1024]{3,0,2,1:T(2,128)(2,1)}, bf16[1,2,64,1024]{3,0,2,1:T(2,128)(2,1)}, u32[]{:S(2)}, u32[]{:S(2)}) collective-permute-start(bf16[1,2,64,1024]{3,0,2,1:T(2,128)(2,1)} %get-tuple-element.214), channel_id=1, source_target_pairs={{0,3},{1,2},{2,1},{3,0},{4,7},{5,6},{6,5},{7,4},{8,11},{9,10},{10,... | collective-permute-start | bytes 786440 | tf_op jit(solution)/shard_map/ppermute | solution.py:27
  231.9 13.5 %copy-start.14 = (bf16[4,2,64,1024]{3,1,2,0:T(2,128)(2,1)S(1)}, bf16[4,2,64,1024]{3,1,2,0:T(2,128)(2,1)}, u32[]{:S(2)}) copy-start(bf16[4,2,64,1024]{3,1,2,0:T(2,128)(2,1)} %copy-done.13) | copy-start | bytes 3145732
  241.2 45.7 %all-to-all-start.1 = ((bf16[128,8,512]{0,2,1:T(8,128)(2,1)}), bf16[128,8,512]{0,2,1:T(8,128)(2,1)}, u32[]{:S(2)}, u32[]{:S(2)}) async-start(bf16[128,8,512]{0,2,1:T(8,128)(2,1)} %bitcast.12), calls=%async_computation.1 | async-start | bytes 2097152 | tf_op jit(solution)/shard_map/all_to_all | solution.py:139
  245.4 110.1 %all-reduce.7.cloned.1.call-start = ((), (), s32[]{:S(2)}) async-start(), calls=%async_computation.12 | async-start | bytes 262144 | tf_op jit(solution)/shard_map/psum | solution.py:210
  281.8 200.7 %all-reduce.9.cloned.1.call-start = ((), (), s32[]{:S(2)}) async-start(), calls=%async_computation.15 | async-start | bytes 786432 | tf_op jit(solution)/shard_map/psum | solution.py:233
  284.8 70.8 %copy-start.20 = (bf16[8,64,512]{2,0,1:T(8,128)(2,1)S(1)}, bf16[8,64,512]{2,0,1:T(8,128)(2,1)}, u32[]{:S(2)}) copy-start(bf16[8,64,512]{2,0,1:T(8,128)(2,1)} %copy-done.19) | copy-start | bytes 1572868
  409.7 72.8 %copy-start.21 = (bf16[1024,64]{0,1:T(8,128)(2,1)S(1)}, bf16[1024,64]{0,1:T(8,128)(2,1)}, u32[]{:S(2)}) copy-start(bf16[1024,64]{0,1:T(8,128)(2,1)} %all-reduce.7.cloned.1.call-done) | copy-start | bytes 393220
  488.6 13.3 %all-to-all-start.8 = ((bf16[4,2,64,512]{3,1,2,0:T(2,128)(2,1)}), bf16[4,2,64,512]{3,1,2,0:T(2,128)(2,1)}, u32[]{:S(2)}, u32[]{:S(2)}) async-start(bf16[4,2,64,512]{3,1,2,0:T(2,128)(2,1)} %copy.184), calls=%async_computation.8 | async-start | bytes 1048576 | tf_op jit(solution)/shard_map/all_to_all | solution.py:256
  501.9 13.0 %all-to-all-start.10 = ((bf16[4,2,64,512]{3,1,2,0:T(2,128)(2,1)}), bf16[4,2,64,512]{3,1,2,0:T(2,128)(2,1)}, u32[]{:S(2)}, u32[]{:S(2)}) async-start(bf16[4,2,64,512]{3,1,2,0:T(2,128)(2,1)} %copy.190), calls=%async_computation.10 | async-start | bytes 1048576 | tf_op jit(solution)/shard_map/all_to_all | solution.py:263
  514.9 18.0 %all-to-all-start.11 = ((bf16[4,2,64,1024]{3,1,2,0:T(2,128)(2,1)}), bf16[4,2,64,1024]{3,1,2,0:T(2,128)(2,1)S(1)}, u32[]{:S(2)}, u32[]{:S(2)}) async-start(bf16[4,2,64,1024]{3,1,2,0:T(2,128)(2,1)} %copy.195), calls=%async_computation.11 | async-start | bytes 2097152 | tf_op jit(solution)/shard_map/all_to_all | solution.py:270
  532.9 19.0 %all-to-all-start.7 = ((bf16[4,2,64,1024]{3,1,2,0:T(2,128)(2,1)}), bf16[4,2,64,1024]{3,1,2,0:T(2,128)(2,1)}, u32[]{:S(2)}, u32[]{:S(2)}) async-start(bf16[4,2,64,1024]{3,1,2,0:T(2,128)(2,1)} %copy.173), calls=%async_computation.7 | async-start | bytes 2097152 | tf_op jit(solution)/shard_map/all_to_all | solution.py:249
  (21 other events, 100.0 us)
Sparse Core Ops, SparseCore 0:
  128.0 61.6 all-gather.4
  200.1 61.4 all-gather.6
  281.9 73.5 all-reduce.6
  411.3 71.1 all-reduce.8
